TPU v7x, 32 devices: a whole 2x2x4 slice. The times are simulated.
32 devices in a mesh: dp: 8 (over y, x, core), tensor: 4 (over z).
Axes of the slice: x: 2, y: 2, z: 4, core: 2. Of those that a mesh axis runs over, the one named last changes fastest.
Arguments:
- inputs: bfloat16 [8192, 8192], P('dp', 'tensor'), may hold values from -6 to 6
- cotangent: bfloat16 [8192, 8192], P('dp', 'tensor'), may hold values from -6 to 6
- projector: bfloat16 [8192, 512], P('tensor'), may hold values from -0.0625 to 0.0625
- weight: bfloat16 [8192, 8192], P('dp', 'tensor'), may hold values from -6 to 6
- moment: float32 [512, 8192], P('dp', 'tensor'), may hold values from -6 to 6
- second_moment: float32 [512, 8192], P('dp', 'tensor'), may hold values from 0.01 to 1
Outputs:
- new_weight: bfloat16 [8192, 8192], P('dp', 'tensor')
- new_moment: float32 [512, 8192], P('dp', 'tensor')
- new_second: float32 [512, 8192], P('dp', 'tensor')
All inputs are finite; a program needn't handle non-finite values.
Results may differ from a plain program's by a relative error of at most 0.0034.
Values may be sent and summed in bfloat16 or wider, within the bound.
A program may use at most 64 MiB of HBM per device.

v0:
```python
import math

import jax
import jax.numpy as jnp
from jax import lax
from jax.sharding import PartitionSpec as P

STEP = 1000


beta_one = 0.9
beta_two = 0.999
epsilon = 1e-08
step_size = 0.5


def broadcast(value, axis, source):
    kept = jnp.where(lax.axis_index(axis) == source, value, 0).astype(value.dtype)
    return lax.psum(kept, axis)


def on_device(inputs, cotangent, projector, weight, moment, second_moment):
    tensor_count = lax.axis_size("tensor")
    data_count = lax.axis_size("dp")
    partial_sum = jnp.dot(inputs, projector, preferred_element_type=jnp.float32)
    projected = lax.psum(partial_sum, "tensor").astype(jnp.bfloat16)
    scale = 1.0 / math.sqrt(inputs.shape[0] * data_count)
    columns = projected
    gradient = (
        lax.psum_scatter(
            lax.dot_general(
                columns, cotangent, (((0,), (0,)), ((), ())), preferred_element_type=jnp.float32
            ),
            "dp",
            scatter_dimension=0,
            tiled=True,
        )
        * scale
    )
    new_moment = beta_one * moment + (1.0 - beta_one) * gradient
    new_second = beta_two * second_moment + (1.0 - beta_two) * gradient * gradient
    first_fix = 1.0 - beta_one**STEP
    second_fix = 1.0 - beta_two**STEP
    update = (new_moment / first_fix / (jnp.sqrt(new_second / second_fix) + epsilon)).astype(
        jnp.bfloat16
    )
    row_count = weight.shape[0]
    ratio = data_count // tensor_count
    data_index = lax.axis_index("dp")
    source = data_index // ratio
    block = broadcast(projector, "tensor", source)
    own_rows = lax.dynamic_slice_in_dim(block, data_index % ratio * row_count, row_count, 0)
    initial = jnp.zeros((row_count, weight.shape[1]), jnp.float32)
    segment = lax.all_gather(update, "dp", axis=0, tiled=True)
    columns = lax.slice_in_dim(own_rows, 0, segment.shape[0], axis=1)
    expanded = initial + jnp.dot(columns, segment, preferred_element_type=jnp.float32)
    new_weight = (weight.astype(jnp.float32) - step_size * expanded).astype(jnp.bfloat16)
    return (new_weight, new_moment, new_second)


def solution(mesh):
    return jax.shard_map(
        on_device,
        mesh=mesh,
        in_specs=(
            P("dp", "tensor"),
            P("dp", "tensor"),
            P("tensor", None),
            P("dp", "tensor"),
            P("dp", "tensor"),
            P("dp", "tensor"),
        ),
        out_specs=(P("dp", "tensor"), P("dp", "tensor"), P("dp", "tensor")),
        check_vma=False,
    )
```

profile of v0, /device:TPU:7, one launch (start us, length us, event | category | flops | bytes accessed | tf_op | source)
XLA Modules:
  0.0 199.9 jit_solution(12828615039875666143)
XLA Ops:
  8.0 0.0 reduce-scatter.2.cloned.1.call-start
  8.0 5.2 %fusion.4 = f32[1024,512]{1,0:T(8,128)S(1)} fusion(bf16[1024,2048]{1,0:T(8,128)(2,1)} %param.6, bf16[2048,512]{1,0:T(8,128)(2,1)} %param.8), kind=kOutput, calls=%fused_computation.9 | convolution fusion | flops 2147483648 | bytes 8388608 | tf_op jit(solution)/shard_map/dot_general | solution.py:25
  13.2 74.1 %all-reduce.4 = bf16[1024,512]{1,0:T(8,128)(2,1)S(1)} all-reduce(f32[1024,512]{1,0:T(8,128)S(1)} %fusion.4), channel_id=1, replica_groups=mesh['dp'=8,'tensor'=4] {'tensor'}, use_global_device_ids=true, to_apply=%region_1.0 | all-reduce | flops 524288 | bytes 3145728 | tf_op jit(solution)/shard_map/psum | solution.py:26
  87.3 6.6 %fusion.5 = f32[512,2048]{1,0:T(8,128)} fusion(bf16[1024,512]{1,0:T(8,128)(2,1)S(1)} %all-reduce.4, bf16[1024,2048]{1,0:T(8,128)(2,1)} %param.7), kind=kOutput, calls=%fused_computation.10 | convolution fusion | flops 2147483648 | bytes 9437184 | tf_op jit(solution)/shard_map/dot_general | solution.py:31
  93.9 0.0 copy-start
  93.9 0.0 reduce-scatter.2.cloned.1.call-update
  93.9 0.0 copy-start.1
  94.0 0.0 copy-start.2
  94.0 0.0 all-reduce.3.cloned.1.call-start
  94.0 1.5 copy-done
  95.5 1.4 broadcast_select_fusion
  97.0 0.0 all-reduce.3.cloned.1.call-update
  97.0 0.0 all-gather.2.cloned.1.call-start
  97.0 49.7 %reduce-scatter.2.cloned.1.call-done = f32[64,2048]{1,0:T(8,128)} async-done(((f32[512,2048]{1,0:T(8,128)}), f32[64,2048]{1,0:T(8,128)}) %reduce-scatter.2.cloned.1.call-update) | async-done | bytes 524304 | tf_op jit(solution)/shard_map/reduce_scatter | solution.py:30
  146.7 0.0 copy-done.1
  146.7 0.0 copy-done.2
  146.7 2.3 %divide_convert_fusion = (bf16[64,2048]{1,0:T(8,128)(2,1)}, f32[64,2048]{1,0:T(8,128)}, f32[64,2048]{1,0:T(8,128)}) fusion(f32[64,2048]{1,0:T(8,128)} %reduce-scatter.2.cloned.1.call-done, f32[64,2048]{1,0:T(8,128)S(1)} %copy-done.1, f32[64,2048]{1,0:T(8,128)S(1)} %copy-done.2), kind=kLoop, calls=%fused_computation.5 | loop fusion | flops 1572864 | bytes 2883584 | tf_op jit(solution)/shard_map/convert_element_type | solution.py:44
  149.0 0.0 all-gather.2.cloned.1.call-update
  149.0 35.9 %all-reduce.3.cloned.1.call-done = bf16[2048,512]{1,0:T(8,128)(2,1)} async-done(((bf16[2048,512]{1,0:T(8,128)(2,1)}), bf16[2048,512]{1,0:T(8,128)(2,1)}) %all-reduce.3.cloned.1.call-update) | async-done | bytes 2097168 | tf_op jit(solution)/shard_map/psum | solution.py:19
  185.0 0.0 all-gather.2.cloned.1.call-done
  185.0 7.5 %subtract_convert_fusion = bf16[1024,2048]{1,0:T(8,128)(2,1)} fusion(bf16[1024,2048]{1,0:T(8,128)(2,1)} %param.9, bf16[512,2048]{1,0:T(8,128)(2,1)} %all-gather.2.cloned.1.call-done, bf16[2048,512]{1,0:T(8,128)(2,1)} %all-reduce.3.cloned.1.call-done, s32[]{:T(128)S(6)} %select_n.26), kind=kOutput, calls=%fused_computation | convolution fusion | flops 2155872256 | bytes 11534340 | tf_op jit(solution)/shard_map/dot_general | solution.py:56
Async XLA Ops:
  8.0 138.7 %reduce-scatter.2.cloned.1.call-start = ((), (), s32[]{:S(2)}) async-start(), calls=%async_computation.2 | async-start | bytes 4718592 | tf_op jit(solution)/shard_map/reduce_scatter | solution.py:30
  93.9 1.6 copy-start
  93.9 52.8 %copy-start.1 = (f32[64,2048]{1,0:T(8,128)S(1)}, f32[64,2048]{1,0:T(8,128)}, u32[]{:S(2)}) copy-start(f32[64,2048]{1,0:T(8,128)} %param.11) | copy-start | bytes 1572868
  94.0 52.8 %copy-start.2 = (f32[64,2048]{1,0:T(8,128)S(1)}, f32[64,2048]{1,0:T(8,128)}, u32[]{:S(2)}) copy-start(f32[64,2048]{1,0:T(8,128)} %param.10) | copy-start | bytes 1572868
  94.0 91.0 %all-reduce.3.cloned.1.call-start = ((), (), s32[]{:S(2)}) async-start(), calls=%async_computation.1 | async-start | bytes 4194304 | tf_op jit(solution)/shard_map/psum | solution.py:19
  97.0 88.0 %all-gather.2.cloned.1.call-start = ((), (), s32[]{:S(2)}) async-start(), calls=%async_computation.3 | async-start | bytes 2359296 | tf_op jit(solution)/shard_map/all_gather | solution.py:54
Sparse Core Ops, SparseCore 0:
  94.1 52.5 reduce-scatter.1
  149.3 28.2 all-gather.1
Sparse Core Ops, SparseCore 1:
  97.1 87.9 all-reduce.2
where the time goes:
time: 202 us; the launch traced here: 200 us
  waiting for transfers between devices  85.7 us (42%)
  blocking collectives  74.1 us (37%)
  matrix products  19.3 us (10%)
  between operations  15.5 us (8%)
  other arithmetic  3.74 us (2%)
    psum x1, blocking collectives, on_device(): projected = lax.psum(partial_sum, 'tensor').astype(jnp.bfloat16)  74.1 us
    reduce_scatter x1, waiting for transfers between devices, on_device(): lax.psum_scatter(lax.dot_general(columns, cotangent, (((0,), (0,)), ((),...  49.7 us
    psum x1, waiting for transfers between devices, broadcast(): return lax.psum(kept, axis)  35.9 us
    dot_general x1, matrix products, on_device(): jnp.dot(columns, segment, preferred_element_type=jnp.float32)  7.5 us
    dot_general x1, matrix products, on_device(): lax.dot_general(columns, cotangent, (((0,), (0,)), ((), ())), preferred_e...  6.58 us
    dot_general x1, matrix products, on_device(): partial_sum = jnp.dot(inputs, projector, preferred_element_type=jnp.float32)  5.18 us
  transfers between devices with their start and end apart: 3, of which 2 were waited for; matrix products, arithmetic and copies ran while one was open for 2% of the time, Pallas kernels for 0%

commit v1 on v0

v1 whole, which is shorter than its diff:
```python
import math

import jax
import jax.numpy as jnp
from jax import lax
from jax.experimental import pallas as pl
from jax.experimental.pallas import tpu as pltpu
from jax.sharding import PartitionSpec as P

STEP = 1000

beta_one = 0.9
beta_two = 0.999
epsilon = 1e-08
step_size = 0.5

TOKEN_CHUNKS = 8
COLUMN_CHUNKS = 4
BASIS_CHUNKS = 8
MESH = pl.DeviceIdType.MESH


def make_kernel(tensor_count, data_count, tokens, features, rank, rows, columns):
    K, NC, NB = TOKEN_CHUNKS, COLUMN_CHUNKS, BASIS_CHUNKS
    tc, w, br = tokens // K, columns // NC, rows // NB
    r = rank // data_count
    m = data_count // 2
    half = tensor_count // 2
    ratio = features // rows
    scale = 1.0 / math.sqrt(tokens * data_count)
    first_fix = 1.0 - beta_one**STEP
    second_fix = 1.0 - beta_two**STEP

    def kernel(
        x_hbm, c_hbm, p_hbm, w_hbm, m_hbm, v_hbm,
        out, new_m, new_v,
        x, cot, proj, wt, mom, sec,
        sfull, zsend, zrecv, exrecv, projd, grad,
        sibsend, sibrecv, own, cssend, csrecv, upd, basis,
        x_sem, l_sem, in_s, in_r, ex_s, ex_r, out_s, out_r,
        sib_s, sib_r, cs_s, cs_r, up_s, up_r, fw_s, fw_r,
        dn_s, dn_r, hi_s, hi_r,
    ):
        t = lax.axis_index("tensor")
        i = lax.axis_index("dp")
        n = tensor_count
        parity = lax.rem(i, 2)
        chip = lax.div(i, 2)
        sibling = i + 1 - 2 * parity
        lower = t < half
        tin = jnp.where(lower, t + 1, t - 1)
        tout = jnp.where(lower, t - 1, t + 1)
        dist = jnp.where(lower, half - 1 - t, t - half)
        is_ex = dist == 0
        has_outer = dist < half - 1
        lag = 1 + 5 * dist
        source = lax.div(i, ratio)
        part = lax.rem(i, ratio)

        def local(k, src, dst):
            return pltpu.make_async_copy(src, dst, l_sem.at[k])

        def xload(k):
            return pltpu.make_async_copy(
                x_hbm.at[pl.ds(k * tc, tc)], x.at[pl.ds(k * tc, tc)], x_sem.at[k]
            )

        loads = [
            local(0, p_hbm, proj),
            local(1, c_hbm, cot),
            local(2, m_hbm, mom),
            local(3, v_hbm, sec),
            local(4, w_hbm, wt),
        ]
        loads[0].start()
        for k in range(K):
            xload(k).start()
        for load in loads[1:]:
            load.start()

        barrier = pltpu.get_barrier_semaphore()

        @pl.when(t > 0)
        def _():
            pl.semaphore_signal(barrier, inc=1, device_id={"tensor": t - 1}, device_id_type=MESH)

        @pl.when(t < n - 1)
        def _():
            pl.semaphore_signal(barrier, inc=1, device_id={"tensor": t + 1}, device_id_type=MESH)

        pl.semaphore_signal(barrier, inc=1, device_id={"dp": sibling}, device_id_type=MESH)
        for d in range(1, m):
            peer = 2 * lax.rem(chip + d, m) + parity
            pl.semaphore_signal(barrier, inc=1, device_id={"dp": peer}, device_id_type=MESH)

        def remote(src, dst, send, recv, where):
            return pltpu.make_async_remote_copy(
                src_ref=src, dst_ref=dst, send_sem=send, recv_sem=recv,
                device_id=where, device_id_type=MESH,
            )

        def inward(k):
            return remote(zsend.at[k], zrecv.at[k], in_s.at[k], in_r.at[k], {"tensor": tin})

        def exchange(k):
            return remote(zsend.at[k], exrecv.at[k], ex_s.at[k], ex_r.at[k], {"tensor": tin})

        def outward(k):
            return remote(projd.at[k], projd.at[k], out_s.at[k], out_r.at[k], {"tensor": tout})

        def basis_down(k):
            return remote(basis.at[k], basis.at[k], dn_s.at[k], dn_r.at[k], {"tensor": t - 1})

        def basis_up(k):
            return remote(basis.at[k], basis.at[k], hi_s.at[k], hi_r.at[k], {"tensor": t + 1})

        def product(k):
            xload(k).wait()
            sfull[k] = jnp.dot(
                x[pl.ds(pl.multiple_of(k * tc, tc), tc), :],
                proj[...],
                preferred_element_type=jnp.float32,
            )

        loads[0].wait()
        product(0)
        grad[...] = jnp.zeros_like(grad)
        pl.semaphore_wait(
            barrier, m + jnp.where(t > 0, 1, 0) + jnp.where(t < n - 1, 1, 0)
        )
        loads[1].wait()

        def reduce_step(k):
            @pl.when(has_outer)
            def _():
                inward(k).wait_recv()
                sfull[k] = sfull[k] + zrecv[k].astype(jnp.float32)

            zsend[k] = sfull[k].astype(jnp.bfloat16)

            @pl.when(is_ex)
            def _():
                exchange(k).start()

            @pl.when(jnp.logical_not(is_ex))
            def _():
                inward(k).start()

        def total_step(k):
            @pl.when(is_ex)
            def _():
                exchange(k).wait_recv()
                projd[k] = (sfull[k] + exrecv[k].astype(jnp.float32)).astype(jnp.bfloat16)

            @pl.when(jnp.logical_not(is_ex))
            def _():
                outward(k).wait_recv()

            @pl.when(has_outer)
            def _():
                outward(k).start()

            def tile(q, carry):
                cols = pl.ds(pl.multiple_of(q * w, w), w)
                grad[:, cols] += lax.dot_general(
                    projd[k],
                    cot[pl.ds(pl.multiple_of(k * tc, tc), tc), cols],
                    (((0,), (0,)), ((), ())),
                    preferred_element_type=jnp.float32,
                )
                return carry

            lax.fori_loop(0, NC, tile, 0)

        def z_step(s, carry):
            @pl.when(s + 1 < K)
            def _():
                product(s + 1)

            @pl.when(s < K)
            def _():
                reduce_step(s)

            @pl.when(jnp.logical_and(s >= lag, s < lag + K))
            def _():
                total_step(s - lag)

            return carry

        lax.fori_loop(0, K + 1 + 5 * (half - 1), z_step, 0)

        @pl.when(t == source)
        def _():
            def send(k, carry):
                basis[k] = proj[pl.ds(pl.multiple_of(part * rows + k * br, br), br), :]

                @pl.when(t > 0)
                def _():
                    basis_down(k).start()

                @pl.when(t < n - 1)
                def _():
                    basis_up(k).start()

                return carry

            lax.fori_loop(0, NB, send, 0)

        def basis_step(k):
            @pl.when(t < source)
            def _():
                basis_down(k).wait_recv()

                @pl.when(t > 0)
                def _():
                    basis_down(k).start()

            @pl.when(t > source)
            def _():
                basis_up(k).wait_recv()

                @pl.when(t < n - 1)
                def _():
                    basis_up(k).start()

        def to_sibling(q):
            return remote(
                sibsend.at[q], sibrecv.at[q], sib_s.at[q], sib_r.at[q], {"dp": sibling}
            )

        def to_chip(q, d):
            peer = 2 * lax.rem(chip + d, m) + parity
            return remote(
                cssend.at[q, d], csrecv.at[q, d], cs_s.at[q, d], cs_r.at[q, d], {"dp": peer}
            )

        def block(owner):
            return pl.ds(pl.multiple_of(owner * r, r), r)

        def update_to_chip(q, d):
            peer = 2 * lax.rem(chip + d, m) + parity
            return remote(
                upd.at[q, block(i)], upd.at[q, block(i)], up_s.at[q, d], up_r.at[q, d],
                {"dp": peer},
            )

        def update_to_sibling(q, d):
            owner = 2 * lax.rem(chip - d + m, m) + parity
            return remote(
                upd.at[q, block(owner)], upd.at[q, block(owner)], fw_s.at[q, d], fw_r.at[q, d],
                {"dp": sibling},
            )

        def sibling_step(q, carry):
            cols = pl.ds(pl.multiple_of(q * w, w), w)
            for j in range(m):
                sibsend[q, j] = grad[block(2 * j + 1 - parity), cols].astype(jnp.bfloat16)
            to_sibling(q).start()
            return carry

        lax.fori_loop(0, NC, sibling_step, 0)

        def chip_step(q, carry):
            cols = pl.ds(pl.multiple_of(q * w, w), w)
            to_sibling(q).wait_recv()
            for d in range(1, m):
                j = lax.rem(chip + d, m)
                cssend[q, d] = (
                    grad[block(2 * j + parity), cols] + sibrecv[q, j].astype(jnp.float32)
                ).astype(jnp.bfloat16)
                to_chip(q, d).start()
            own[q] = grad[block(i), cols] + sibrecv[q, chip].astype(jnp.float32)
            return carry

        lax.fori_loop(0, NC, chip_step, 0)
        loads[2].wait()
        loads[3].wait()

        def adam_step(q, carry):
            cols = pl.ds(pl.multiple_of(q * w, w), w)

            @pl.when(q >= 1)
            def _():
                basis_step(q - 1)

            total = own[q]
            for d in range(1, m):
                to_chip(q, d).wait_recv()
                total = total + csrecv[q, d].astype(jnp.float32)
            gradient = total * scale
            moment = beta_one * mom[:, cols] + (1.0 - beta_one) * gradient
            second = beta_two * sec[:, cols] + (1.0 - beta_two) * gradient * gradient
            new_m[:, cols] = moment
            new_v[:, cols] = second
            upd[q, block(i)] = (
                moment / first_fix / (jnp.sqrt(second / second_fix) + epsilon)
            ).astype(jnp.bfloat16)
            for d in range(1, m):
                update_to_chip(q, d).start()
            update_to_sibling(q, 0).start()
            return carry

        lax.fori_loop(0, NC, adam_step, 0)

        def gather_step(q, carry):
            basis_step(q + NC - 1)
            for d in range(1, m):
                update_to_chip(q, d).wait_recv()
                update_to_sibling(q, d).start()
            return carry

        lax.fori_loop(0, NC, gather_step, 0)
        for k in range(2 * NC - 1, NB):
            basis_step(k)

        loads[4].wait()

        def sibling_wait(q, carry):
            for d in range(m):
                owner = 2 * lax.rem(chip - d + m, m) + 1 - parity
                remote(
                    upd.at[q, block(owner)], upd.at[q, block(owner)],
                    fw_s.at[q, d], fw_r.at[q, d], {"dp": sibling},
                ).wait_recv()
            return carry

        lax.fori_loop(0, NC, sibling_wait, 0)

        def final(q, carry):
            cols = pl.ds(pl.multiple_of(q * w, w), w)

            def row_step(k, carry):
                lines = pl.ds(pl.multiple_of(k * br, br), br)
                expanded = jnp.dot(basis[k], upd[q], preferred_element_type=jnp.float32)
                out[lines, cols] = (
                    wt[lines, cols].astype(jnp.float32) - step_size * expanded
                ).astype(jnp.bfloat16)
                return carry

            return lax.fori_loop(0, NB, row_step, carry)

        lax.fori_loop(0, NC, final, 0)

        def drain_z(k, carry):
            @pl.when(is_ex)
            def _():
                exchange(k).wait_send()

            @pl.when(jnp.logical_not(is_ex))
            def _():
                inward(k).wait_send()

            @pl.when(has_outer)
            def _():
                outward(k).wait_send()

            return carry

        lax.fori_loop(0, K, drain_z, 0)

        def drain_basis(k, carry):
            @pl.when(jnp.logical_and(t <= source, t > 0))
            def _():
                basis_down(k).wait_send()

            @pl.when(jnp.logical_and(t >= source, t < n - 1))
            def _():
                basis_up(k).wait_send()

            return carry

        lax.fori_loop(0, NB, drain_basis, 0)

        def drain_dp(q, carry):
            to_sibling(q).wait_send()
            update_to_sibling(q, 0).wait_send()
            for d in range(1, m):
                to_chip(q, d).wait_send()
                update_to_chip(q, d).wait_send()
                update_to_sibling(q, d).wait_send()
            return carry

        lax.fori_loop(0, NC, drain_dp, 0)

    dma = pltpu.SemaphoreType.DMA
    bf16, f32 = jnp.bfloat16, jnp.float32
    scratch = [
        pltpu.VMEM((tokens, features), bf16),
        pltpu.VMEM((tokens, columns), bf16),
        pltpu.VMEM((features, rank), bf16),
        pltpu.VMEM((rows, columns), bf16),
        pltpu.VMEM((r, columns), f32),
        pltpu.VMEM((r, columns), f32),
        pltpu.VMEM((K, tc, rank), f32),
        pltpu.VMEM((K, tc, rank), bf16),
        pltpu.VMEM((K, tc, rank), bf16),
        pltpu.VMEM((K, tc, rank), bf16),
        pltpu.VMEM((K, tc, rank), bf16),
        pltpu.VMEM((rank, columns), f32),
        pltpu.VMEM((NC, m, r, w), bf16),
        pltpu.VMEM((NC, m, r, w), bf16),
        pltpu.VMEM((NC, r, w), f32),
        pltpu.VMEM((NC, m, r, w), bf16),
        pltpu.VMEM((NC, m, r, w), bf16),
        pltpu.VMEM((NC, rank, w), bf16),
        pltpu.VMEM((NB, br, rank), bf16),
        dma((K,)),
        dma((5,)),
        *[dma((K,))] * 6,
        *[dma((NC,))] * 2,
        *[dma((NC, m))] * 6,
        *[dma((NB,))] * 4,
    ]
    return kernel, scratch


def solution(mesh):
    tensor_count, data_count = mesh.shape["tensor"], mesh.shape["dp"]

    def on_device(inputs, cotangent, projector, weight, moment, second_moment):
        tokens, features = inputs.shape
        rank = projector.shape[1]
        rows, columns = weight.shape
        kernel, scratch = make_kernel(
            tensor_count, data_count, tokens, features, rank, rows, columns
        )
        return pl.pallas_call(
            kernel,
            out_shape=(
                jax.ShapeDtypeStruct(weight.shape, weight.dtype),
                jax.ShapeDtypeStruct(moment.shape, moment.dtype),
                jax.ShapeDtypeStruct(second_moment.shape, second_moment.dtype),
            ),
            in_specs=[pl.BlockSpec(memory_space=pl.ANY)] * 6,
            out_specs=tuple([pl.BlockSpec(memory_space=pltpu.VMEM)] * 3),
            scratch_shapes=scratch,
            compiler_params=pltpu.CompilerParams(
                collective_id=0, has_side_effects=True, vmem_limit_bytes=60 * 1024 * 1024
            ),
        )(inputs, cotangent, projector, weight, moment, second_moment)

    return jax.shard_map(
        on_device,
        mesh=mesh,
        in_specs=(
            P("dp", "tensor"),
            P("dp", "tensor"),
            P("tensor", None),
            P("dp", "tensor"),
            P("dp", "tensor"),
            P("dp", "tensor"),
        ),
        out_specs=(P("dp", "tensor"), P("dp", "tensor"), P("dp", "tensor")),
        check_vma=False,
    )
```

time: 202 us -> 95.4 us (0.47)
  Pallas kernels: 0 us -> 88.1 us
  waiting for transfers between devices: 85.7 us -> 0 us
  blocking collectives: 74.1 us -> 0 us
  matrix products: 19.3 us -> 0 us
  between operations: 15.5 us -> 0.66 us
  local copies, waits for them, and re-layouts: 1.49 us -> 6.47 us
  other arithmetic: 3.74 us -> 0 us
    pallas_call x0 -> x1, Pallas kernels: none -> 88.1 us  [on_device(): pl.pallas_call(kernel, out_shape=(jax.ShapeDtypeStruct(weight.shape, weig...]
    psum x1 -> x0, blocking collectives: 74.1 us -> none  [on_device(): projected = lax.psum(partial_sum, 'tensor').astype(jnp.bfloat16)]
    reduce_scatter x1 -> x0, waiting for transfers between devices: 49.7 us -> none  [on_device(): lax.psum_scatter(lax.dot_general(columns, cotangent, (((0,), (0,)), ((),...]
    psum x1 -> x0, waiting for transfers between devices: 35.9 us -> none  [broadcast(): return lax.psum(kept, axis)]
    dot_general x3 -> x0, matrix products: 19.3 us -> none  [the longest x1 7.5 us: on_device(): jnp.dot(columns, segment, preferred_element_type=jnp.float32)]
    unnamed x6 -> x7, local copies, waits for them, and re-layouts: 1.49 us -> 6.47 us
    convert_element_type x1 -> x0, other arithmetic: 2.29 us -> none  [on_device(): (new_moment / first_fix / (jnp.sqrt(new_second / second_fix) + epsilon))....]
  transfers between devices with their start and end apart: 3 -> 0, of which waited for: 2 -> 0; matrix products, arithmetic and copies ran while one was open for 2% -> 0% of each run, Pallas kernels for 0% -> 0%
where the time goes in v1:
time: 95.4 us; the launch traced here: 95.2 us
  Pallas kernels  88.1 us (92%)
  local copies, waits for them, and re-layouts  6.47 us (7%)
    pallas_call x1, Pallas kernels, on_device(): pl.pallas_call(kernel, out_shape=(jax.ShapeDtypeStruct(weight.shape, weig...  88.1 us
    unnamed x7, local copies, waits for them, and re-layouts  6.47 us

profile of v1, /device:TPU:7, one launch (start us, length us, event | category | flops | bytes accessed | tf_op | source)
XLA Modules:
  0.0 95.2 jit_solution(4553807724207450659)
XLA Ops:
  0.6 88.1 %shard_map.85 = (bf16[1024,2048]{1,0:T(8,128)(2,1)}, f32[64,2048]{1,0:T(8,128)}, f32[64,2048]{1,0:T(8,128)}) custom-call(bf16[1024,2048]{1,0:T(8,128)(2,1)} %x_hbm.1, bf16[1024,2048]{1,0:T(8,128)(2,1)} %c_hbm.1, bf16[2048,512]{1,0:T(8,128)(2,1)} %p_hbm.1, bf16[1024,2048]{1,0:T(8,128)(2,1)} %w_hbm.1, f32[64,2048]{1,0:T(8,128)} %m_hbm.1, f32[64,2048]{1,0:T(8,128)} %v_hbm.1), custom_call_target="tpu_custom_call" | custom-call | tf_op jit(solution)/shard_map/pallas_call | solution.py:427
  88.7 0.0 copy-start.1
  88.7 0.0 copy-start
  88.7 4.9 %copy.12 = bf16[1024,2048]{1,0:T(8,128)(2,1)} copy(bf16[1024,2048]{1,0:T(8,128)(2,1)} %get-tuple-element.6) | data formatting | bytes 8388608
  93.6 0.0 copy-done.1
  93.6 0.8 copy.13
  94.4 0.0 copy-done
  94.4 0.8 copy.14
Async XLA Ops:
  88.7 4.9 %copy-start.1 = (f32[64,2048]{1,0:T(8,128)S(1)}, f32[64,2048]{1,0:T(8,128)}, u32[]{:S(2)}) copy-start(f32[64,2048]{1,0:T(8,128)} %get-tuple-element.7) | copy-start | bytes 1572868
  88.7 5.7 %copy-start = (f32[64,2048]{1,0:T(8,128)S(1)}, f32[64,2048]{1,0:T(8,128)}, u32[]{:S(2)}) copy-start(f32[64,2048]{1,0:T(8,128)} %get-tuple-element.8) | copy-start | bytes 1572868

commit v2 on v1

--- a/solution.py
+++ b/solution.py
@@ -14,7 +14,10 @@
 epsilon = 1e-08
 step_size = 0.5
 
-TOKEN_CHUNKS = 8
+TOKEN_CHUNKS = 16
+GROUP = 2
+LAG = 3
+HOP_LAG = 7
 COLUMN_CHUNKS = 4
 BASIS_CHUNKS = 8
 MESH = pl.DeviceIdType.MESH
@@ -23,6 +26,7 @@
 def make_kernel(tensor_count, data_count, tokens, features, rank, rows, columns):
     K, NC, NB = TOKEN_CHUNKS, COLUMN_CHUNKS, BASIS_CHUNKS
     tc, w, br = tokens // K, columns // NC, rows // NB
+    tg = tc * GROUP
     r = rank // data_count
     m = data_count // 2
     half = tensor_count // 2
@@ -32,9 +36,9 @@
     second_fix = 1.0 - beta_two**STEP
 
     def kernel(
-        x_hbm, c_hbm, p_hbm, w_hbm, m_hbm, v_hbm,
-        out, new_m, new_v,
-        x, cot, proj, wt, mom, sec,
+        x_hbm, c_hbm, p_hbm, m_hbm, v_hbm,
+        upd_out, basis_out, new_m, new_v,
+        x, cot, proj, mom, sec,
         sfull, zsend, zrecv, exrecv, projd, grad,
         sibsend, sibrecv, own, cssend, csrecv, upd, basis,
         x_sem, l_sem, in_s, in_r, ex_s, ex_r, out_s, out_r,
@@ -53,7 +57,7 @@
         dist = jnp.where(lower, half - 1 - t, t - half)
         is_ex = dist == 0
         has_outer = dist < half - 1
-        lag = 1 + 5 * dist
+        lag = LAG + HOP_LAG * dist
         source = lax.div(i, ratio)
         part = lax.rem(i, ratio)
 
@@ -62,7 +66,7 @@
 
         def xload(k):
             return pltpu.make_async_copy(
-                x_hbm.at[pl.ds(k * tc, tc)], x.at[pl.ds(k * tc, tc)], x_sem.at[k]
+                x_hbm.at[pl.ds(k * tg, tg)], x.at[pl.ds(k * tg, tg)], x_sem.at[k]
             )
 
         loads = [
@@ -70,10 +74,9 @@
             local(1, c_hbm, cot),
             local(2, m_hbm, mom),
             local(3, v_hbm, sec),
-            local(4, w_hbm, wt),
         ]
         loads[0].start()
-        for k in range(K):
+        for k in range(K // GROUP):
             xload(k).start()
         for load in loads[1:]:
             load.start()
@@ -99,14 +102,20 @@
                 device_id=where, device_id_type=MESH,
             )
 
+        def span(k):
+            return pl.ds(pl.multiple_of(k * tc, tc), tc)
+
+        def group(k):
+            return pl.ds(pl.multiple_of(k * tg, tg), tg)
+
         def inward(k):
-            return remote(zsend.at[k], zrecv.at[k], in_s.at[k], in_r.at[k], {"tensor": tin})
+            return remote(zsend.at[span(k)], zrecv.at[span(k)], in_s.at[k], in_r.at[k], {"tensor": tin})
 
         def exchange(k):
-            return remote(zsend.at[k], exrecv.at[k], ex_s.at[k], ex_r.at[k], {"tensor": tin})
+            return remote(zsend.at[span(k)], exrecv.at[span(k)], ex_s.at[k], ex_r.at[k], {"tensor": tin})
 
         def outward(k):
-            return remote(projd.at[k], projd.at[k], out_s.at[k], out_r.at[k], {"tensor": tout})
+            return remote(projd.at[span(k)], projd.at[span(k)], out_s.at[k], out_r.at[k], {"tensor": tout})
 
         def basis_down(k):
             return remote(basis.at[k], basis.at[k], dn_s.at[k], dn_r.at[k], {"tensor": t - 1})
@@ -116,8 +125,8 @@
 
         def product(k):
             xload(k).wait()
-            sfull[k] = jnp.dot(
-                x[pl.ds(pl.multiple_of(k * tc, tc), tc), :],
+            sfull[group(k)] = jnp.dot(
+                x[group(k), :],
                 proj[...],
                 preferred_element_type=jnp.float32,
             )
@@ -134,9 +143,9 @@
             @pl.when(has_outer)
             def _():
                 inward(k).wait_recv()
-                sfull[k] = sfull[k] + zrecv[k].astype(jnp.float32)
-
-            zsend[k] = sfull[k].astype(jnp.bfloat16)
+                sfull[span(k)] = sfull[span(k)] + zrecv[span(k)].astype(jnp.float32)
+
+            zsend[span(k)] = sfull[span(k)].astype(jnp.bfloat16)
 
             @pl.when(is_ex)
             def _():
@@ -150,7 +159,9 @@
             @pl.when(is_ex)
             def _():
                 exchange(k).wait_recv()
-                projd[k] = (sfull[k] + exrecv[k].astype(jnp.float32)).astype(jnp.bfloat16)
+                projd[span(k)] = (
+                    sfull[span(k)] + exrecv[span(k)].astype(jnp.float32)
+                ).astype(jnp.bfloat16)
 
             @pl.when(jnp.logical_not(is_ex))
             def _():
@@ -160,22 +171,26 @@
             def _():
                 outward(k).start()
 
-            def tile(q, carry):
-                cols = pl.ds(pl.multiple_of(q * w, w), w)
-                grad[:, cols] += lax.dot_general(
-                    projd[k],
-                    cot[pl.ds(pl.multiple_of(k * tc, tc), tc), cols],
-                    (((0,), (0,)), ((), ())),
-                    preferred_element_type=jnp.float32,
-                )
-                return carry
-
-            lax.fori_loop(0, NC, tile, 0)
+            @pl.when(lax.rem(k, GROUP) == GROUP - 1)
+            def _():
+                tokens_now = group(lax.div(k, GROUP))
+
+                def tile(q, carry):
+                    cols = pl.ds(pl.multiple_of(q * w, w), w)
+                    grad[:, cols] += lax.dot_general(
+                        projd[tokens_now, :],
+                        cot[tokens_now, cols],
+                        (((0,), (0,)), ((), ())),
+                        preferred_element_type=jnp.float32,
+                    )
+                    return carry
+
+                lax.fori_loop(0, NC, tile, 0)
 
         def z_step(s, carry):
-            @pl.when(s + 1 < K)
-            def _():
-                product(s + 1)
+            @pl.when(jnp.logical_and(s + GROUP < K, lax.rem(s, GROUP) == 0))
+            def _():
+                product(lax.div(s, GROUP) + 1)
 
             @pl.when(s < K)
             def _():
@@ -187,7 +202,7 @@
 
             return carry
 
-        lax.fori_loop(0, K + 1 + 5 * (half - 1), z_step, 0)
+        lax.fori_loop(0, K + LAG + HOP_LAG * (half - 1), z_step, 0)
 
         @pl.when(t == source)
         def _():
@@ -313,8 +328,6 @@
         for k in range(2 * NC - 1, NB):
             basis_step(k)
 
-        loads[4].wait()
-
         def sibling_wait(q, carry):
             for d in range(m):
                 owner = 2 * lax.rem(chip - d + m, m) + 1 - parity
@@ -326,20 +339,10 @@
 
         lax.fori_loop(0, NC, sibling_wait, 0)
 
-        def final(q, carry):
-            cols = pl.ds(pl.multiple_of(q * w, w), w)
-
-            def row_step(k, carry):
-                lines = pl.ds(pl.multiple_of(k * br, br), br)
-                expanded = jnp.dot(basis[k], upd[q], preferred_element_type=jnp.float32)
-                out[lines, cols] = (
-                    wt[lines, cols].astype(jnp.float32) - step_size * expanded
-                ).astype(jnp.bfloat16)
-                return carry
-
-            return lax.fori_loop(0, NB, row_step, carry)
-
-        lax.fori_loop(0, NC, final, 0)
+        upd_copy = pltpu.make_async_copy(upd, upd_out, l_sem.at[0])
+        upd_copy.start()
+        basis_copy = pltpu.make_async_copy(basis, basis_out, l_sem.at[1])
+        basis_copy.start()
 
         def drain_z(k, carry):
             @pl.when(is_ex)
@@ -381,6 +384,8 @@
             return carry
 
         lax.fori_loop(0, NC, drain_dp, 0)
+        upd_copy.wait()
+        basis_copy.wait()
 
     dma = pltpu.SemaphoreType.DMA
     bf16, f32 = jnp.bfloat16, jnp.float32
@@ -388,14 +393,13 @@
         pltpu.VMEM((tokens, features), bf16),
         pltpu.VMEM((tokens, columns), bf16),
         pltpu.VMEM((features, rank), bf16),
-        pltpu.VMEM((rows, columns), bf16),
         pltpu.VMEM((r, columns), f32),
         pltpu.VMEM((r, columns), f32),
-        pltpu.VMEM((K, tc, rank), f32),
-        pltpu.VMEM((K, tc, rank), bf16),
-        pltpu.VMEM((K, tc, rank), bf16),
-        pltpu.VMEM((K, tc, rank), bf16),
-        pltpu.VMEM((K, tc, rank), bf16),
+        pltpu.VMEM((tokens, rank), f32),
+        pltpu.VMEM((tokens, rank), bf16),
+        pltpu.VMEM((tokens, rank), bf16),
+        pltpu.VMEM((tokens, rank), bf16),
+        pltpu.VMEM((tokens, rank), bf16),
         pltpu.VMEM((rank, columns), f32),
         pltpu.VMEM((NC, m, r, w), bf16),
         pltpu.VMEM((NC, m, r, w), bf16),
@@ -404,8 +408,8 @@
         pltpu.VMEM((NC, m, r, w), bf16),
         pltpu.VMEM((NC, rank, w), bf16),
         pltpu.VMEM((NB, br, rank), bf16),
-        dma((K,)),
-        dma((5,)),
+        dma((K // GROUP,)),
+        dma((4,)),
         *[dma((K,))] * 6,
         *[dma((NC,))] * 2,
         *[dma((NC, m))] * 6,
@@ -424,20 +428,61 @@
         kernel, scratch = make_kernel(
             tensor_count, data_count, tokens, features, rank, rows, columns
         )
+        any_space = pl.BlockSpec(memory_space=pl.ANY)
+        in_vmem = pl.BlockSpec(memory_space=pltpu.VMEM)
+        width, height = columns // COLUMN_CHUNKS, rows // BASIS_CHUNKS
+        update, basis, moment, second_moment = pl.pallas_call(
+            kernel,
+            out_shape=(
+                jax.ShapeDtypeStruct((COLUMN_CHUNKS, rank, width), jnp.bfloat16),
+                jax.ShapeDtypeStruct((BASIS_CHUNKS, height, rank), jnp.bfloat16),
+                jax.ShapeDtypeStruct(moment.shape, moment.dtype),
+                jax.ShapeDtypeStruct(second_moment.shape, second_moment.dtype),
+            ),
+            in_specs=[any_space] * 5,
+            out_specs=(any_space, any_space, in_vmem, in_vmem),
+            scratch_shapes=scratch,
+            compiler_params=pltpu.CompilerParams(
+                collective_id=0, has_side_effects=True, vmem_limit_bytes=60 * 1024 * 1024
+            ),
+        )(inputs, cotangent, projector, moment, second_moment)
+        basis = basis.reshape(rows, rank)
+        tiles = 4
+        line = rows // tiles
+
+        def finish(w_ref, b_ref, u_ref, m_ref, v_ref, out_ref, m_out, v_out):
+            for q in range(COLUMN_CHUNKS):
+                cols = slice(q * width, (q + 1) * width)
+                expanded = jnp.dot(b_ref[...], u_ref[q], preferred_element_type=jnp.float32)
+                out_ref[:, cols] = (
+                    w_ref[:, cols].astype(jnp.float32) - step_size * expanded
+                ).astype(jnp.bfloat16)
+
+            @pl.when(pl.program_id(0) == 0)
+            def _():
+                m_out[...] = m_ref[...]
+                v_out[...] = v_ref[...]
+
+        state = pl.BlockSpec(moment.shape, lambda k: (0, 0))
+        tile = pl.BlockSpec((line, columns), lambda k: (k, 0))
         return pl.pallas_call(
-            kernel,
+            finish,
+            grid=(tiles,),
             out_shape=(
                 jax.ShapeDtypeStruct(weight.shape, weight.dtype),
                 jax.ShapeDtypeStruct(moment.shape, moment.dtype),
                 jax.ShapeDtypeStruct(second_moment.shape, second_moment.dtype),
             ),
-            in_specs=[pl.BlockSpec(memory_space=pl.ANY)] * 6,
-            out_specs=tuple([pl.BlockSpec(memory_space=pltpu.VMEM)] * 3),
-            scratch_shapes=scratch,
-            compiler_params=pltpu.CompilerParams(
-                collective_id=0, has_side_effects=True, vmem_limit_bytes=60 * 1024 * 1024
-            ),
-        )(inputs, cotangent, projector, weight, moment, second_moment)
+            in_specs=[
+                tile,
+                pl.BlockSpec((line, rank), lambda k: (k, 0)),
+                pl.BlockSpec(update.shape, lambda k: (0, 0, 0)),
+                state,
+                state,
+            ],
+            out_specs=(tile, state, state),
+            compiler_params=pltpu.CompilerParams(vmem_limit_bytes=60 * 1024 * 1024),
+        )(weight, basis, update, moment, second_moment)
 
     return jax.shard_map(
         on_device,

time: 95.4 us -> 84.3 us (0.88)
  local copies, waits for them, and re-layouts: 6.47 us -> 0 us
  Pallas kernels: 88.1 us -> 83.5 us
    unnamed x7 -> x0, local copies, waits for them, and re-layouts: 6.47 us -> none
    pallas_call x1 -> x2, Pallas kernels: 88.1 us -> 83.5 us  [the longest x1 75.9 us: on_device(): pl.pallas_call(kernel, out_shape=(jax.ShapeDtypeStruct((COLUMN_CHUNKS, ra...]
where the time goes in v2:
time: 84.3 us; the launch traced here: 84.1 us
  Pallas kernels  83.5 us (99%)
    pallas_call x1, Pallas kernels, on_device(): pl.pallas_call(kernel, out_shape=(jax.ShapeDtypeStruct((COLUMN_CHUNKS, ra...  75.9 us
    pallas_call x1, Pallas kernels, on_device(): pl.pallas_call(finish, grid=(tiles,), out_shape=(jax.ShapeDtypeStruct(wei...  7.58 us

profile of v2, /device:TPU:7, one launch (start us, length us, event | category | flops | bytes accessed | tf_op | source)
XLA Modules:
  0.0 84.1 jit_solution(17396134120342918054)
XLA Ops:
  0.6 75.9 %shard_map.85 = (bf16[4,512,512]{2,1,0:T(8,128)(2,1)}, bf16[8,128,512]{2,1,0:T(8,128)(2,1)}, f32[64,2048]{1,0:T(8,128)}, f32[64,2048]{1,0:T(8,128)}) custom-call(bf16[1024,2048]{1,0:T(8,128)(2,1)} %x_hbm.1, bf16[1024,2048]{1,0:T(8,128)(2,1)} %c_hbm.1, bf16[2048,512]{1,0:T(8,128)(2,1)} %p_hbm.1, f32[64,2048]{1,0:T(8,128)} %m_hbm.1, f32[64,2048]{1,0:T(8,128)} %v_hbm.1), custom_call_target="tpu_custom_call" | custom-call | tf_op jit(solution)/shard_map/pallas_call | solution.py:434
  76.6 7.6 %shard_map.86 = (bf16[1024,2048]{1,0:T(8,128)(2,1)}, f32[64,2048]{1,0:T(8,128)}, f32[64,2048]{1,0:T(8,128)}) custom-call(bf16[1024,2048]{1,0:T(8,128)(2,1)} %w_ref.1, bf16[1024,512]{1,0:T(8,128)(2,1)} %bitcast.1, bf16[4,512,512]{2,1,0:T(8,128)(2,1)} %get-tuple-element.8.u_ref, f32[64,2048]{1,0:T(8,128)} %get-tuple-element.9.m_ref, ...), custom_call_target="tpu_custom_call" | custom-call | tf_op jit(solution)/shard_map/pallas_call | solution.py:468

commit v3 on v2

--- a/solution.py
+++ b/solution.py
@@ -187,25 +187,7 @@
 
                 lax.fori_loop(0, NC, tile, 0)
 
-        def z_step(s, carry):
-            @pl.when(jnp.logical_and(s + GROUP < K, lax.rem(s, GROUP) == 0))
-            def _():
-                product(lax.div(s, GROUP) + 1)
-
-            @pl.when(s < K)
-            def _():
-                reduce_step(s)
-
-            @pl.when(jnp.logical_and(s >= lag, s < lag + K))
-            def _():
-                total_step(s - lag)
-
-            return carry
-
-        lax.fori_loop(0, K + LAG + HOP_LAG * (half - 1), z_step, 0)
-
-        @pl.when(t == source)
-        def _():
+        def send_basis():
             def send(k, carry):
                 basis[k] = proj[pl.ds(pl.multiple_of(part * rows + k * br, br), br), :]
 
@@ -220,6 +202,29 @@
                 return carry
 
             lax.fori_loop(0, NB, send, 0)
+
+        is_source = t == source
+
+        def z_step(s, carry):
+            @pl.when(jnp.logical_and(s + GROUP < K, lax.rem(s, GROUP) == 0))
+            def _():
+                product(lax.div(s, GROUP) + 1)
+
+            @pl.when(s < K)
+            def _():
+                reduce_step(s)
+
+            @pl.when(jnp.logical_and(is_source, s == jnp.where(has_outer, lag + K, K)))
+            def _():
+                send_basis()
+
+            @pl.when(jnp.logical_and(s >= lag, s < lag + K))
+            def _():
+                total_step(s - lag)
+
+            return carry
+
+        lax.fori_loop(0, K + LAG + HOP_LAG * (half - 1) + 1, z_step, 0)
 
         def basis_step(k):
             @pl.when(t < source)
@@ -294,9 +299,7 @@
         def adam_step(q, carry):
             cols = pl.ds(pl.multiple_of(q * w, w), w)
 
-            @pl.when(q >= 1)
-            def _():
-                basis_step(q - 1)
+            basis_step(q)
 
             total = own[q]
             for d in range(1, m):
@@ -318,14 +321,14 @@
         lax.fori_loop(0, NC, adam_step, 0)
 
         def gather_step(q, carry):
-            basis_step(q + NC - 1)
+            basis_step(q + NC)
             for d in range(1, m):
                 update_to_chip(q, d).wait_recv()
                 update_to_sibling(q, d).start()
             return carry
 
         lax.fori_loop(0, NC, gather_step, 0)
-        for k in range(2 * NC - 1, NB):
+        for k in range(2 * NC, NB):
             basis_step(k)
 
         def sibling_wait(q, carry):

time: 84.3 us -> 81.2 us (0.963)
  Pallas kernels: 83.5 us -> 80.4 us
    pallas_call x1, Pallas kernels: 75.9 us -> 72.8 us  [on_device(): pl.pallas_call(kernel, out_shape=(jax.ShapeDtypeStruct((COLUMN_CHUNKS, ra...]
where the time goes in v3:
time: 81.2 us; the launch traced here: 81 us
  Pallas kernels  80.4 us (99%)
    pallas_call x1, Pallas kernels, on_device(): pl.pallas_call(kernel, out_shape=(jax.ShapeDtypeStruct((COLUMN_CHUNKS, ra...  72.8 us
    pallas_call x1, Pallas kernels, on_device(): pl.pallas_call(finish, grid=(tiles,), out_shape=(jax.ShapeDtypeStruct(wei...  7.58 us

profile of v3, /device:TPU:7, one launch (start us, length us, event | category | flops | bytes accessed | tf_op | source)
XLA Modules:
  0.0 81.0 jit_solution(8283829423634853871)
XLA Ops:
  0.6 72.8 %shard_map.85 = (bf16[4,512,512]{2,1,0:T(8,128)(2,1)}, bf16[8,128,512]{2,1,0:T(8,128)(2,1)}, f32[64,2048]{1,0:T(8,128)}, f32[64,2048]{1,0:T(8,128)}) custom-call(bf16[1024,2048]{1,0:T(8,128)(2,1)} %x_hbm.1, bf16[1024,2048]{1,0:T(8,128)(2,1)} %c_hbm.1, bf16[2048,512]{1,0:T(8,128)(2,1)} %p_hbm.1, f32[64,2048]{1,0:T(8,128)} %m_hbm.1, f32[64,2048]{1,0:T(8,128)} %v_hbm.1), custom_call_target="tpu_custom_call" | custom-call | tf_op jit(solution)/shard_map/pallas_call | solution.py:437
  73.4 7.6 %shard_map.86 = (bf16[1024,2048]{1,0:T(8,128)(2,1)}, f32[64,2048]{1,0:T(8,128)}, f32[64,2048]{1,0:T(8,128)}) custom-call(bf16[1024,2048]{1,0:T(8,128)(2,1)} %w_ref.1, bf16[1024,512]{1,0:T(8,128)(2,1)} %bitcast.1, bf16[4,512,512]{2,1,0:T(8,128)(2,1)} %get-tuple-element.8.u_ref, f32[64,2048]{1,0:T(8,128)} %get-tuple-element.9.m_ref, ...), custom_call_target="tpu_custom_call" | custom-call | tf_op jit(solution)/shard_map/pallas_call | solution.py:471
